TPU v7x, 512 devices: a whole 4x4x16 slice. The times are simulated.
512 devices in a mesh: row: 32 (over z_lo, y), col: 16 (over z_hi, x, core).
Axes of the slice: x: 4, y: 4, z: 16 (z_hi: 2, z_lo: 8; z = z_hi * 8 + z_lo), core: 2. Of those that a mesh axis runs over, the one named last changes fastest.
Arguments:
- entries: int32 [128, 64, 128, 128], P('row', 'col'), may hold values from -2 to 2
- tile_cols: int32 [128, 64], P('row', 'col'), may hold values from 0 to 31
- block_now: int32 [32, 65536], P(None, ('col', 'row')), may hold values from 0 to 65520
- block_prev: int32 [32, 65536], P(None, ('col', 'row')), may hold values from 0 to 65520
- block_prev2: int32 [32, 65536], P(None, ('col', 'row')), may hold values from 0 to 65520
- gram_prev: int32 [32, 32], replicated, may hold values from 0 to 65520
- square_prev: int32 [32, 32], replicated, may hold values from 0 to 65520
- inverse_prev: int32 [32, 32], replicated, may hold values from 0 to 65520
- inverse_prev2: int32 [32, 32], replicated, may hold values from 0 to 65520
Outputs:
- next_block: float32 [32, 65536], P(None, ('col', 'row'))
- later_block: float32 [32, 65536], P(None, ('col', 'row'))
Inputs may be any that keep to these rules, and one draw needn't show every extreme that they name: `tile_cols`: stored tiles that name the same tile column in one tile row add. `block_prev`: residues. `block_prev2`: residues. `gram_prev`: residues. `square_prev`: residues. `inverse_prev`: residues. `inverse_prev2`: residues.
All inputs are finite; a program needn't handle non-finite values.
Results may differ from a plain program's by a relative error of at most 0.0003.
Values sent between devices are 32-bit elements; how exact they have to be, the bound alone decides.
No kernel may reach another device: no remote copies, remote signals or barrier semaphores. Data moves between devices by JAX's collectives and lax.ppermute only.
A program may use at most 64 MiB of HBM per device.

v0:
```python
import jax
import jax.numpy as jnp
from jax import lax
from jax.sharding import PartitionSpec as P

modulus = 65521.0


def residue(values):
    return jnp.mod(values, modulus)


def split_digits(values):
    top_part = jnp.floor(values / 256.0)
    return (top_part, values - top_part * 256.0)


def fold_digits(top_sum, low_sum):
    return residue(residue(residue(top_sum) * 256.0) + residue(low_sum))


def fold_three(upper_part, middle, lower_part):
    return residue(
        residue(residue(upper_part) * 15.0) + residue(residue(middle) * 256.0) + residue(lower_part)
    )


def mulmod(left_side, right_side):
    top_part, low_part = split_digits(right_side)
    return fold_digits(left_side * top_part, left_side * low_part)


def exact_dot(left_side, right_side):
    return jnp.dot(
        left_side, right_side, precision=lax.Precision.HIGHEST, preferred_element_type=jnp.float32
    )


def small_product(left_side, right_side):
    left_top, left_low = split_digits(left_side)
    right_top, right_low = split_digits(right_side)
    return fold_three(
        exact_dot(left_top, right_top),
        exact_dot(left_top, right_low) + exact_dot(left_low, right_top),
        exact_dot(left_low, right_low),
    )


def inverse_scalar(number):
    result = jnp.ones_like(number)
    square = number
    exponent = 65519
    for position in range(16):
        if exponent >> position & 1:
            result = mulmod(result, square)
        square = mulmod(square, square)
    return result


def inverse_matrix(matrix):
    matrix_order = matrix.shape[0]
    augmented = jnp.concatenate([matrix, jnp.eye(matrix_order, dtype=matrix.dtype)], axis=1)
    row_numbers = jnp.arange(matrix_order, dtype=jnp.int32)

    def eliminate(column, augmented):
        column = jnp.asarray(column).astype(jnp.int32)
        pivot_column = augmented[:, column]
        usable = (pivot_column != 0.0) & (row_numbers >= column)
        pivot_row_id = jnp.where(jnp.any(usable), jnp.argmax(usable), column)
        pivot_row = augmented[pivot_row_id]
        current_row = augmented[column]
        swapped = jnp.where(
            (row_numbers == column)[:, None],
            pivot_row[None, :],
            jnp.where((row_numbers == pivot_row_id)[:, None], current_row[None, :], augmented),
        )
        scaled = mulmod(pivot_row, inverse_scalar(pivot_row[column]))
        factors = jnp.where(row_numbers == column, 0.0, swapped[:, column])
        reduced = residue(swapped - mulmod(factors[:, None], scaled[None, :]) + modulus)
        return jnp.where((row_numbers == column)[:, None], scaled[None, :], reduced)

    augmented = lax.fori_loop(0, matrix_order, eliminate, augmented)
    return augmented[:, matrix_order:]


def coefficients(
    gram_now, square_now, inverse_now, inverse_prev, inverse_prev2, gram_old, square_old
):
    identity = jnp.eye(gram_now.shape[0], dtype=gram_now.dtype)
    first = residue(identity - small_product(residue(square_now + gram_now), inverse_now) + modulus)
    second = residue(modulus - small_product(gram_now, inverse_prev))
    middle = residue(identity - small_product(inverse_prev, gram_old) + modulus)
    third = residue(
        modulus
        - small_product(small_product(residue(square_old + gram_old), middle), inverse_prev2)
    )
    return jnp.concatenate([first, second, third], axis=1)


def digit_stack(values):
    top_part, low_part = split_digits(values)
    return jnp.stack([top_part, low_part]).astype(jnp.bfloat16)


def combine_blocks(coeffs, stacked):
    products = jnp.einsum(
        "dab,ebn->dean",
        digit_stack(coeffs),
        digit_stack(stacked),
        preferred_element_type=jnp.float32,
    )
    return fold_three(products[0, 0], products[0, 1] + products[1, 0], products[1, 1])


def gram_local(first, second):
    column_count = first.shape[1]
    group_width = min(column_count, 128)
    groups = column_count // group_width
    first_digits = digit_stack(first).reshape(2, first.shape[0], groups, group_width)
    second_digits = digit_stack(second).reshape(2, second.shape[0], groups, group_width)
    products = jnp.einsum(
        "dagw,ecgw->gdeac", first_digits, second_digits, preferred_element_type=jnp.float32
    )
    per_group = fold_three(
        products[:, 0, 0], products[:, 0, 1] + products[:, 1, 0], products[:, 1, 1]
    )
    return residue(jnp.sum(per_group, axis=0))


def digit_pair(values):
    top_part, low_part = split_digits(values)
    return jnp.stack([top_part, low_part])


def forward_partial(block_full, tile_values, tile_cols):
    tile_rows, slot_count, tile_size = (
        tile_values.shape[0],
        tile_values.shape[1],
        tile_values.shape[2],
    )
    block_rows = block_full.shape[0]
    top_part, low_part = split_digits(block_full)
    digits = jnp.concatenate([top_part, low_part], axis=0).astype(jnp.bfloat16)
    digits = digits.reshape(2 * block_rows, -1, tile_size)
    picked = jnp.take(digits, tile_cols.reshape(-1), axis=1).reshape(
        2 * block_rows, tile_rows, slot_count, tile_size
    )
    raw_sums = jnp.einsum("brsk,rsjk->brj", picked, tile_values, preferred_element_type=jnp.float32)
    return fold_digits(raw_sums[:block_rows], raw_sums[block_rows:]).reshape(
        block_rows, tile_rows * tile_size
    )


def backward_partial(projected, tile_values, onehot):
    tile_rows, tile_size = (tile_values.shape[0], tile_values.shape[2])
    block_rows = projected.shape[0]
    top_part, low_part = split_digits(projected)
    digits = (
        jnp.concatenate([top_part, low_part], axis=0)
        .astype(jnp.bfloat16)
        .reshape(2 * block_rows, tile_rows, tile_size)
    )
    spread = jnp.einsum("brj,rsjk->brsk", digits, tile_values, preferred_element_type=jnp.float32)
    raw_sums = jnp.einsum(
        "brsk,rsc->bck",
        spread,
        onehot,
        precision=lax.Precision.HIGHEST,
        preferred_element_type=jnp.float32,
    )
    return fold_digits(raw_sums[:block_rows], raw_sums[block_rows:]).reshape(block_rows, -1)


def body(
    entries,
    tile_cols,
    block_now,
    block_prev,
    block_prev2,
    gram_prev,
    square_prev,
    inverse_prev,
    inverse_prev2,
):
    tile_values = entries.astype(jnp.bfloat16)
    tile_size = tile_values.shape[2]
    share_width = block_now.shape[1]
    col_tiles = share_width * lax.axis_size("row") // tile_size
    onehot = (
        tile_cols[:, :, None] == jnp.arange(col_tiles, dtype=jnp.int32)[None, None, :]
    ).astype(jnp.float32)
    current = block_now.astype(jnp.float32)
    earlier = block_prev.astype(jnp.float32)
    earliest = block_prev2.astype(jnp.float32)
    gram_old = gram_prev.astype(jnp.float32)
    square_old = square_prev.astype(jnp.float32)
    inverse_old = inverse_prev.astype(jnp.float32)
    inverse_older = inverse_prev2.astype(jnp.float32)
    results = []
    for iteration in range(2):
        block_full = lax.all_gather(current, "row", axis=1, tiled=True)
        projected = residue(lax.psum(forward_partial(block_full, tile_values, tile_cols), "col"))
        partial_term = backward_partial(projected, tile_values, onehot)
        applied = residue(lax.psum_scatter(partial_term, "row", scatter_dimension=1, tiled=True))
        current_own = current
        both_sums = lax.psum(
            jnp.stack(
                [
                    digit_pair(gram_local(current_own, applied)),
                    digit_pair(gram_local(applied, applied)),
                ]
            ),
            ("row", "col"),
        )
        gram_now = fold_digits(both_sums[0, 0], both_sums[0, 1])
        square_now = fold_digits(both_sums[1, 0], both_sums[1, 1])
        inverse_now = inverse_matrix(gram_now)
        coeffs = coefficients(
            gram_now, square_now, inverse_now, inverse_old, inverse_older, gram_old, square_old
        )
        stacked = jnp.concatenate([current, earlier, earliest], axis=0)
        following = residue(applied + combine_blocks(coeffs, stacked))
        results.append(following / modulus)
        earliest, earlier, current = (earlier, current, following)
        inverse_older, inverse_old = (inverse_old, inverse_now)
        gram_old, square_old = (gram_now, square_now)
    return (results[0], results[1])


def solution(mesh):
    placed = (
        P("row", "col", None, None),
        P("row", "col"),
        P(None, ("col", "row")),
        P(None, ("col", "row")),
        P(None, ("col", "row")),
        P(),
        P(),
        P(),
        P(),
    )
    return jax.shard_map(
        body,
        mesh=mesh,
        in_specs=placed,
        out_specs=(P(None, ("col", "row")), P(None, ("col", "row"))),
        check_vma=False,
    )
```

profile of v0, /device:TPU:1, one launch (start us, length us, event | category | flops | bytes accessed | tf_op | source)
XLA Modules:
  0.0 2244.6 jit_solution(948067549384732013)
XLA Ops:
  7.2 0.8 reshape.1652
  8.8 114.7 %all_gather.6 = f32[32,4096]{1,0:T(8,128)S(1)} all-gather(f32[32,128]{1,0:T(8,128)S(1)} %get-tuple-element.319), channel_id=1, replica_groups=mesh['row'=32,'col'=16] {'row'}, dimensions={1}, use_global_device_ids=true | all-gather | bytes 540672 | tf_op jit(solution)/shard_map/all_gather | solution.py:201
  124.9 0.8 copy_bitcast_fusion.7
  129.3 247.2 %all-reduce.3.cloned.1.call-done = f32[32,512]{1,0:T(8,128)} async-done(((f32[32,512]{1,0:T(8,128)}), f32[32,512]{1,0:T(8,128)}) %all-reduce.3.cloned.1.call-update) | async-done | bytes 65552 | tf_op jit(solution)/shard_map/psum | solution.py:202
  376.5 0.9 fusion.102
  378.1 1.1 convolution_bitcast_fusion.1
  379.2 1.1 add_select_fusion.22
  380.3 1.1 copy.355
  383.5 212.7 %reduce-scatter.3.cloned.1.call-done = f32[32,128]{1,0:T(8,128)} async-done(((f32[32,4096]{1,0:T(8,128)}), f32[32,128]{1,0:T(8,128)}) %reduce-scatter.3.cloned.1.call-update) | async-done | bytes 16400 | tf_op jit(solution)/shard_map/reduce_scatter | solution.py:204
  596.2 0.7 fusion.339
  597.5 125.4 %psum.29 = f32[2,2,32,32]{2,3,1,0:T(8,128)S(1)} all-reduce(f32[2,2,32,32]{2,3,1,0:T(8,128)S(1)} %pad_maximum_fusion.2), channel_id=1, replica_groups=mesh['row'=32,'col'=16] {'row','col'}, use_global_device_ids=true, to_apply=%region_2.4 | all-reduce | flops 4096 | bytes 32768 | tf_op jit(solution)/shard_map/psum | solution.py:206
  722.9 403.5 %while.36 = (s32[]{:T(128)}, f32[32,64]{0,1:T(8,128)S(1)}, s32[]{:T(128)}, s32[]{:T(128)}, s32[]{:T(128)}, /*index=5*/s32[]{:T(128)}, s32[]{:T(128)}, f32[]{:T(128)}, f32[]{:T(128)}, f32[]{:T(128)}, /*index=10*/f32[]{:T(128)}) while((s32[]{:T(128)}, f32[32,64]{0,1:T(8,128)S(1)}, s32[]{:T(128)}, s32[]{:T(128)}, ...), condition=%wide.region_6.8_spmd.clone.clone, body=%wide.region_3.7_spmd.clone.clone.sunk | while | flops 87498 | bytes 50118 | solution.py:82
  723.6 0.7 iota_reduce_fusion.4
  736.2 0.7 iota_reduce_fusion.4
  748.8 0.7 iota_reduce_fusion.4
  761.4 0.7 iota_reduce_fusion.4
  774.0 0.7 iota_reduce_fusion.4
  786.7 0.7 iota_reduce_fusion.4
  799.3 0.7 iota_reduce_fusion.4
  811.9 0.7 iota_reduce_fusion.4
  824.5 0.7 iota_reduce_fusion.4
  837.1 0.7 iota_reduce_fusion.4
  849.7 0.7 iota_reduce_fusion.4
  862.3 0.7 iota_reduce_fusion.4
  874.9 0.7 iota_reduce_fusion.4
  887.5 0.7 iota_reduce_fusion.4
  900.1 0.7 iota_reduce_fusion.4
  912.7 0.7 iota_reduce_fusion.4
  925.3 0.7 iota_reduce_fusion.4
  938.0 0.7 iota_reduce_fusion.4
  950.6 0.7 iota_reduce_fusion.4
  963.2 0.7 iota_reduce_fusion.4
  975.8 0.7 iota_reduce_fusion.4
  988.4 0.7 iota_reduce_fusion.4
  1001.0 0.7 iota_reduce_fusion.4
  1013.6 0.7 iota_reduce_fusion.4
  1026.2 0.7 iota_reduce_fusion.4
  1038.8 0.7 iota_reduce_fusion.4
  1076.7 0.7 iota_reduce_fusion.4
  1101.9 0.7 iota_reduce_fusion.4
  1114.5 0.7 iota_reduce_fusion.4
  1129.8 103.1 %all_gather.7 = f32[32,4096]{1,0:T(8,128)S(1)} all-gather(f32[32,128]{1,0:T(8,128)S(1)} %get-tuple-element.280), channel_id=1, replica_groups=mesh['row'=32,'col'=16] {'row'}, dimensions={1}, use_global_device_ids=true | all-gather | bytes 540672 | tf_op jit(solution)/shard_map/all_gather | solution.py:201
  1234.2 0.8 copy_bitcast_fusion.6
  1235.6 249.9 %all-reduce.5.cloned.1.call-done = f32[32,512]{1,0:T(8,128)} async-done(((f32[32,512]{1,0:T(8,128)}), f32[32,512]{1,0:T(8,128)}) %all-reduce.5.cloned.1.call-update) | async-done | bytes 65552 | tf_op jit(solution)/shard_map/psum | solution.py:202
  1485.5 0.9 fusion.103
  1486.7 1.1 convolution_bitcast_fusion
  1487.7 1.1 add_select_fusion.18
  1488.9 1.1 copy.354
  1491.4 213.1 %reduce-scatter.5.cloned.1.call-done = f32[32,128]{1,0:T(8,128)} async-done(((f32[32,4096]{1,0:T(8,128)}), f32[32,128]{1,0:T(8,128)}) %reduce-scatter.5.cloned.1.call-update) | async-done | bytes 16400 | tf_op jit(solution)/shard_map/reduce_scatter | solution.py:204
  1704.5 0.7 fusion.343
  1705.8 125.7 %psum.31 = f32[2,2,32,32]{2,3,1,0:T(8,128)S(1)} all-reduce(f32[2,2,32,32]{2,3,1,0:T(8,128)S(1)} %pad_maximum_fusion.3), channel_id=1, replica_groups=mesh['row'=32,'col'=16] {'row','col'}, use_global_device_ids=true, to_apply=%region_9.11 | all-reduce | flops 4096 | bytes 32768 | tf_op jit(solution)/shard_map/psum | solution.py:206
  1831.6 403.5 %while.37 = (s32[]{:T(128)}, f32[32,64]{0,1:T(8,128)S(1)}, s32[]{:T(128)}, s32[]{:T(128)}, s32[]{:T(128)}, /*index=5*/s32[]{:T(128)}, s32[]{:T(128)}, f32[]{:T(128)}, f32[]{:T(128)}, f32[]{:T(128)}, /*index=10*/f32[]{:T(128)}) while((s32[]{:T(128)}, f32[32,64]{0,1:T(8,128)S(1)}, s32[]{:T(128)}, s32[]{:T(128)}, ...), condition=%wide.region_13.15_spmd.clone.clone, body=%wide.region_10.14_spmd.clone.clone.sunk | while | flops 87498 | bytes 50118 | solution.py:82
  1832.2 0.7 iota_reduce_fusion.5
  1844.8 0.7 iota_reduce_fusion.5
  1983.5 0.7 iota_reduce_fusion.5
  1996.1 0.7 iota_reduce_fusion.5
  2008.8 0.7 iota_reduce_fusion.5
  2021.4 0.7 iota_reduce_fusion.5
  2034.0 0.7 iota_reduce_fusion.5
  2046.6 0.7 iota_reduce_fusion.5
  2059.2 0.7 iota_reduce_fusion.5
  2071.8 0.7 iota_reduce_fusion.5
  2084.4 0.7 iota_reduce_fusion.5
  2223.1 0.7 iota_reduce_fusion.5
  (674 shorter events, 155.7 us)
Async XLA Ops:
  7.2 116.5 %copy-start = (s32[4,4,128,128]{3,2,1,0:T(8,128)S(1)}, s32[4,4,128,128]{3,2,1,0:T(8,128)}, u32[]{:S(2)}) copy-start(s32[4,4,128,128]{3,2,1,0:T(8,128)} %param.15) | copy-start | bytes 3145732
  7.2 369.3 %all-reduce.3.cloned.1.call-start = ((), (), s32[]{:S(2)}) async-start(), calls=%async_computation.2 | async-start | bytes 131072 | tf_op jit(solution)/shard_map/psum | solution.py:202
  125.7 0.7 copy-start.5
  125.7 0.8 copy-start.6
  125.7 470.4 %reduce-scatter.3.cloned.1.call-start = ((), (), s32[]{:S(2)}) async-start(), calls=%async_computation.3 | async-start | bytes 540672 | tf_op jit(solution)/shard_map/reduce_scatter | solution.py:204
  126.9 0.7 copy-start.7
  128.2 0.7 copy-start.8
  377.4 0.7 copy-start.4
  381.5 1104.0 %all-reduce.5.cloned.1.call-start = ((), (), s32[]{:S(2)}) async-start(), calls=%async_computation.4 | async-start | bytes 131072 | tf_op jit(solution)/shard_map/psum | solution.py:202
  382.0 0.7 copy-start.9
  382.0 0.7 copy-start.10
  382.8 0.7 copy-start.1
  1129.0 0.7 copy-start.2
  1235.0 469.5 %reduce-scatter.5.cloned.1.call-start = ((), (), s32[]{:S(2)}) async-start(), calls=%async_computation.5 | async-start | bytes 540672 | tf_op jit(solution)/shard_map/reduce_scatter | solution.py:204
  2236.6 0.7 copy-start.3
Sparse Core Ops, SparseCore 0:
  125.8 250.6 all-reduce.2
  381.6 214.5 reduce-scatter.2
  1235.1 250.3 all-reduce.4
  1490.1 214.3 reduce-scatter.4
where the time goes:
time: 2250 us; the launch traced here: 2240 us
  waiting for transfers between devices  923 us (41%)
  loops' own time  641 us (28%)
  blocking collectives  469 us (21%)
  other arithmetic  139 us (6%)
  local copies, waits for them, and re-layouts  47.5 us (2%)
    another operation x2, loops' own time, inverse_matrix(): augmented = lax.fori_loop(0, matrix_order, eliminate, augmented)  641 us
    psum x2, waiting for transfers between devices, body(): lax.psum(forward_partial(block_full, tile_values, tile_cols), 'col')  497 us
    reduce_scatter x2, waiting for transfers between devices, body(): lax.psum_scatter(partial_term, 'row', scatter_dimension=1, tiled=True)  426 us
    psum x2, blocking collectives, body(): lax.psum(jnp.stack([digit_pair(gram_local(current_own, applied)), digit_p...  251 us
    all_gather x2, blocking collectives, body(): block_full = lax.all_gather(current, 'row', axis=1, tiled=True)  218 us
    another operation x64, other arithmetic, eliminate(): pivot_row_id = jnp.where(jnp.any(usable), jnp.argmax(usable), column)  46.5 us
  transfers between devices with their start and end apart: 4, of which 4 were waited for; matrix products, arithmetic and copies ran while one was open for 0% of the time, Pallas kernels for 0%

commit v1 on v0

--- a/solution.py
+++ b/solution.py
@@ -204,13 +204,16 @@
         applied = residue(lax.psum_scatter(partial_term, "row", scatter_dimension=1, tiled=True))
         current_own = current
         both_sums = lax.psum(
-            jnp.stack(
-                [
-                    digit_pair(gram_local(current_own, applied)),
-                    digit_pair(gram_local(applied, applied)),
-                ]
+            lax.psum(
+                jnp.stack(
+                    [
+                        digit_pair(gram_local(current_own, applied)),
+                        digit_pair(gram_local(applied, applied)),
+                    ]
+                ),
+                "col",
             ),
-            ("row", "col"),
+            "row",
         )
         gram_now = fold_digits(both_sums[0, 0], both_sums[0, 1])
         square_now = fold_digits(both_sums[1, 0], both_sums[1, 1])

time: 2250 us -> 2740 us (1.22); the launches traced: 2240 us -> 2700 us
  blocking collectives: 469 us -> 880 us
  waiting for transfers between devices: 923 us -> 967 us
    psum x0 -> x2, blocking collectives: none -> 394 us  [body(): lax.psum(lax.psum(jnp.stack([digit_pair(gram_local(current_own, applied))...]
    psum x2, waiting for transfers between devices: 497 us -> 541 us  [body(): lax.psum(forward_partial(block_full, tile_values, tile_cols), 'col')]
where the time goes in v1:
time: 2740 us; the launch traced here: 2700 us
  waiting for transfers between devices  967 us (35%)
  blocking collectives  880 us (32%)
  loops' own time  641 us (23%)
  other arithmetic  139 us (5%)
  local copies, waits for them, and re-layouts  47.5 us (2%)
    another operation x2, loops' own time, inverse_matrix(): augmented = lax.fori_loop(0, matrix_order, eliminate, augmented)  641 us
    psum x2, waiting for transfers between devices, body(): lax.psum(forward_partial(block_full, tile_values, tile_cols), 'col')  541 us
    reduce_scatter x2, waiting for transfers between devices, body(): lax.psum_scatter(partial_term, 'row', scatter_dimension=1, tiled=True)  426 us
    psum x2, blocking collectives, body(): lax.psum(lax.psum(jnp.stack([digit_pair(gram_local(current_own, applied))...  394 us
    psum x2, blocking collectives, body(): lax.psum(jnp.stack([digit_pair(gram_local(current_own, applied)), digit_p...  271 us
    all_gather x2, blocking collectives, body(): block_full = lax.all_gather(current, 'row', axis=1, tiled=True)  215 us
  transfers between devices with their start and end apart: 4, of which 4 were waited for; matrix products, arithmetic and copies ran while one was open for 0% of the time, Pallas kernels for 0%

profile of v1, /device:TPU:1, one launch (start us, length us, event | category | flops | bytes accessed | tf_op | source)
XLA Modules:
  0.0 2699.5 jit_solution(183661386175523601)
XLA Ops:
  7.2 0.8 reshape.1652
  8.8 114.7 %all_gather.6 = f32[32,4096]{1,0:T(8,128)S(1)} all-gather(f32[32,128]{1,0:T(8,128)S(1)} %get-tuple-element.319), channel_id=1, replica_groups=mesh['row'=32,'col'=16] {'row'}, dimensions={1}, use_global_device_ids=true | all-gather | bytes 540672 | tf_op jit(solution)/shard_map/all_gather | solution.py:201
  124.9 0.8 copy_bitcast_fusion.7
  129.3 247.2 %all-reduce.3.cloned.1.call-done = f32[32,512]{1,0:T(8,128)} async-done(((f32[32,512]{1,0:T(8,128)}), f32[32,512]{1,0:T(8,128)}) %all-reduce.3.cloned.1.call-update) | async-done | bytes 65552 | tf_op jit(solution)/shard_map/psum | solution.py:202
  376.5 0.9 fusion.102
  378.1 1.1 convolution_bitcast_fusion.1
  379.2 1.1 add_select_fusion.22
  380.3 1.1 copy.355
  383.5 212.7 %reduce-scatter.3.cloned.1.call-done = f32[32,128]{1,0:T(8,128)} async-done(((f32[32,4096]{1,0:T(8,128)}), f32[32,128]{1,0:T(8,128)}) %reduce-scatter.3.cloned.1.call-update) | async-done | bytes 16400 | tf_op jit(solution)/shard_map/reduce_scatter | solution.py:204
  596.2 0.7 fusion.339
  597.5 135.6 %psum.43 = f32[2,2,32,32]{2,3,1,0:T(8,128)S(1)} all-reduce(f32[2,2,32,32]{2,3,1,0:T(8,128)S(1)} %pad_maximum_fusion.2), channel_id=1, replica_groups=mesh['row'=32,'col'=16] {'col'}, use_global_device_ids=true, to_apply=%region_2.4 | all-reduce | flops 4096 | bytes 32768 | tf_op jit(solution)/shard_map/psum | solution.py:207
  733.1 197.0 %psum.44 = f32[2,2,32,32]{2,3,1,0:T(8,128)S(1)} all-reduce(f32[2,2,32,32]{2,3,1,0:T(8,128)S(1)} %psum.43), channel_id=1, replica_groups=mesh['row'=32,'col'=16] {'row'}, use_global_device_ids=true, to_apply=%region_3.5 | all-reduce | flops 4096 | bytes 32768 | tf_op jit(solution)/shard_map/psum | solution.py:206
  930.2 403.5 %while.36 = (s32[]{:T(128)}, f32[32,64]{0,1:T(8,128)S(1)}, s32[]{:T(128)}, s32[]{:T(128)}, s32[]{:T(128)}, /*index=5*/s32[]{:T(128)}, s32[]{:T(128)}, f32[]{:T(128)}, f32[]{:T(128)}, f32[]{:T(128)}, /*index=10*/f32[]{:T(128)}) while((s32[]{:T(128)}, f32[32,64]{0,1:T(8,128)S(1)}, s32[]{:T(128)}, s32[]{:T(128)}, ...), condition=%wide.region_7.9_spmd.clone.clone, body=%wide.region_4.8_spmd.clone.clone.sunk | while | flops 87498 | bytes 50118 | solution.py:82
  930.8 0.7 iota_reduce_fusion.4
  943.4 0.7 iota_reduce_fusion.4
  956.1 0.7 iota_reduce_fusion.4
  968.7 0.7 iota_reduce_fusion.4
  981.3 0.7 iota_reduce_fusion.4
  993.9 0.7 iota_reduce_fusion.4
  1006.5 0.7 iota_reduce_fusion.4
  1019.1 0.7 iota_reduce_fusion.4
  1031.7 0.7 iota_reduce_fusion.4
  1044.3 0.7 iota_reduce_fusion.4
  1056.9 0.7 iota_reduce_fusion.4
  1069.5 0.7 iota_reduce_fusion.4
  1082.1 0.7 iota_reduce_fusion.4
  1094.7 0.7 iota_reduce_fusion.4
  1107.4 0.7 iota_reduce_fusion.4
  1120.0 0.7 iota_reduce_fusion.4
  1132.6 0.7 iota_reduce_fusion.4
  1195.6 0.7 iota_reduce_fusion.4
  1208.2 0.7 iota_reduce_fusion.4
  1220.8 0.7 iota_reduce_fusion.4
  1233.4 0.7 iota_reduce_fusion.4
  1246.0 0.7 iota_reduce_fusion.4
  1258.7 0.7 iota_reduce_fusion.4
  1271.3 0.7 iota_reduce_fusion.4
  1283.9 0.7 iota_reduce_fusion.4
  1296.5 0.7 iota_reduce_fusion.4
  1337.0 100.1 %all_gather.7 = f32[32,4096]{1,0:T(8,128)S(1)} all-gather(f32[32,128]{1,0:T(8,128)S(1)} %get-tuple-element.280), channel_id=1, replica_groups=mesh['row'=32,'col'=16] {'row'}, dimensions={1}, use_global_device_ids=true | all-gather | bytes 540672 | tf_op jit(solution)/shard_map/all_gather | solution.py:201
  1438.4 0.8 copy_bitcast_fusion.6
  1439.8 293.5 %all-reduce.5.cloned.1.call-done = f32[32,512]{1,0:T(8,128)} async-done(((f32[32,512]{1,0:T(8,128)}), f32[32,512]{1,0:T(8,128)}) %all-reduce.5.cloned.1.call-update) | async-done | bytes 65552 | tf_op jit(solution)/shard_map/psum | solution.py:202
  1733.3 0.9 fusion.103
  1734.4 1.1 convolution_bitcast_fusion
  1735.5 1.1 add_select_fusion.18
  1736.6 1.1 copy.354
  1739.1 213.3 %reduce-scatter.5.cloned.1.call-done = f32[32,128]{1,0:T(8,128)} async-done(((f32[32,4096]{1,0:T(8,128)}), f32[32,128]{1,0:T(8,128)}) %reduce-scatter.5.cloned.1.call-update) | async-done | bytes 16400 | tf_op jit(solution)/shard_map/reduce_scatter | solution.py:204
  1952.4 0.7 fusion.343
  1953.7 135.7 %psum.46 = f32[2,2,32,32]{2,3,1,0:T(8,128)S(1)} all-reduce(f32[2,2,32,32]{2,3,1,0:T(8,128)S(1)} %pad_maximum_fusion.3), channel_id=1, replica_groups=mesh['row'=32,'col'=16] {'col'}, use_global_device_ids=true, to_apply=%region_10.12 | all-reduce | flops 4096 | bytes 32768 | tf_op jit(solution)/shard_map/psum | solution.py:207
  2089.4 197.0 %psum.47 = f32[2,2,32,32]{2,3,1,0:T(8,128)S(1)} all-reduce(f32[2,2,32,32]{2,3,1,0:T(8,128)S(1)} %psum.46), channel_id=1, replica_groups=mesh['row'=32,'col'=16] {'row'}, use_global_device_ids=true, to_apply=%region_11.13 | all-reduce | flops 4096 | bytes 32768 | tf_op jit(solution)/shard_map/psum | solution.py:206
  2286.5 403.5 %while.37 = (s32[]{:T(128)}, f32[32,64]{0,1:T(8,128)S(1)}, s32[]{:T(128)}, s32[]{:T(128)}, s32[]{:T(128)}, /*index=5*/s32[]{:T(128)}, s32[]{:T(128)}, f32[]{:T(128)}, f32[]{:T(128)}, f32[]{:T(128)}, /*index=10*/f32[]{:T(128)}) while((s32[]{:T(128)}, f32[32,64]{0,1:T(8,128)S(1)}, s32[]{:T(128)}, s32[]{:T(128)}, ...), condition=%wide.region_15.17_spmd.clone.clone, body=%wide.region_12.16_spmd.clone.clone.sunk | while | flops 87498 | bytes 50118 | solution.py:82
  2287.1 0.7 iota_reduce_fusion.5
  2299.7 0.7 iota_reduce_fusion.5
  2312.3 0.7 iota_reduce_fusion.5
  2325.0 0.7 iota_reduce_fusion.5
  2463.6 0.7 iota_reduce_fusion.5
  2476.3 0.7 iota_reduce_fusion.5
  2488.9 0.7 iota_reduce_fusion.5
  2501.5 0.7 iota_reduce_fusion.5
  2514.1 0.7 iota_reduce_fusion.5
  2526.7 0.7 iota_reduce_fusion.5
  2539.3 0.7 iota_reduce_fusion.5
  2551.9 0.7 iota_reduce_fusion.5
  2564.5 0.7 iota_reduce_fusion.5
  (676 shorter events, 157.1 us)
Async XLA Ops:
  7.2 116.5 %copy-start = (s32[4,4,128,128]{3,2,1,0:T(8,128)S(1)}, s32[4,4,128,128]{3,2,1,0:T(8,128)}, u32[]{:S(2)}) copy-start(s32[4,4,128,128]{3,2,1,0:T(8,128)} %param.15) | copy-start | bytes 3145732
  7.2 369.3 %all-reduce.3.cloned.1.call-start = ((), (), s32[]{:S(2)}) async-start(), calls=%async_computation.2 | async-start | bytes 131072 | tf_op jit(solution)/shard_map/psum | solution.py:202
  125.7 0.7 copy-start.5
  125.7 0.8 copy-start.6
  125.7 470.4 %reduce-scatter.3.cloned.1.call-start = ((), (), s32[]{:S(2)}) async-start(), calls=%async_computation.3 | async-start | bytes 540672 | tf_op jit(solution)/shard_map/reduce_scatter | solution.py:204
  126.9 0.7 copy-start.7
  128.2 0.7 copy-start.8
  377.4 0.7 copy-start.4
  381.5 1351.8 %all-reduce.5.cloned.1.call-start = ((), (), s32[]{:S(2)}) async-start(), calls=%async_computation.4 | async-start | bytes 131072 | tf_op jit(solution)/shard_map/psum | solution.py:202
  382.0 0.7 copy-start.9
  382.0 0.7 copy-start.10
  382.8 0.7 copy-start.1
  1336.2 0.7 copy-start.2
  1439.2 513.2 %reduce-scatter.5.cloned.1.call-start = ((), (), s32[]{:S(2)}) async-start(), calls=%async_computation.5 | async-start | bytes 540672 | tf_op jit(solution)/shard_map/reduce_scatter | solution.py:204
  2691.5 0.7 copy-start.3
Sparse Core Ops, SparseCore 0:
  125.8 250.6 all-reduce.2
  381.6 214.5 reduce-scatter.2
  1439.3 293.9 all-reduce.4
  1737.9 214.5 reduce-scatter.4
